TPU v7x, 256 devices: a whole 4x4x8 slice. The times are simulated.
256 devices in a mesh: row: 8 (over y, x_hi), col: 32 (over z, x_lo, core).
Axes of the slice: x: 4 (x_hi: 2, x_lo: 2; x = x_hi * 2 + x_lo), y: 4, z: 8, core: 2. Of those that a mesh axis runs over, the one named last changes fastest.
Arguments:
- query_proj: bfloat16 [128, 1536, 128], P('row', 'col'), may hold values from -6 to 6
- key_proj: bfloat16 [128, 1536, 128], P('row', 'col'), may hold values from -6 to 6
- value_proj: bfloat16 [128, 1536, 128], P('row', 'col'), may hold values from -6 to 6
- attn_out: bfloat16 [128, 1536, 128], P('row', 'col'), may hold values from -6 to 6
- out_grad: bfloat16 [128, 1536, 128], P('row', 'col'), may hold values from -6 to 6
- log_norm: float32 [4, 128, 1536], P(None, 'row', 'col'), may hold values from 3 to 5
- pair_mask: int32 [128, 1536], P('row'), may hold values 0 or 1
- pair_bias: bfloat16 [4, 1536, 1536], P(None, 'col', 'row'), may hold values from -6 to 6
Outputs:
- query_grad: bfloat16 [128, 1536, 128], P('row', 'col')
- key_grad: bfloat16 [128, 1536, 128], P('row', 'col')
- value_grad: bfloat16 [128, 1536, 128], P('row', 'col')
- bias_grad: bfloat16 [4, 1536, 1536], P(None, 'col', 'row')
All inputs are finite; a program needn't handle non-finite values. No bound on the sum of `pair_mask` on one device may be relied on, other than what follows from the above.
Results may differ from a plain program's by a relative error of at most 0.0051.
Values may be sent and summed in bfloat16 or wider, within the bound.
A program may use at most 192 MiB of HBM per device.

v0:
```python
import functools

import jax
import jax.numpy as jnp
from jax import lax
from jax.experimental import pallas as pl
from jax.experimental.pallas import tpu as pltpu
from jax.sharding import PartitionSpec as P

MESH = pl.DeviceIdType.MESH
HEADS = 4
BIG = 1.0e30
F32 = jnp.float32
BF16 = jnp.bfloat16
NT = (((1,), (1,)), ((), ()))
TN = (((0,), (0,)), ((), ()))


def iota(shape, axis):
    return lax.broadcasted_iota(jnp.int32, shape, axis)


def split3(value):
    high = value.astype(BF16).astype(F32)
    rest = value - high
    middle = rest.astype(BF16).astype(F32)
    low = (rest - middle).astype(BF16).astype(F32)
    return high, middle, low


def kernel(
    geometry, scaling,
    q_ref, k_ref, v_ref, o_ref, g_ref, ln_ref, mask_ref, bias_ref,
    dq_out, dk_out, dv_out, db_out,
    o_own, g_own, ln_own, mask_own, bias_own, bias_wide,
    qg, st, st_out, kx, vx, ws, wp, ws_t, wp_t, bias_all,
    acc_in, acc_out, dq_own, dk_acc, dv_acc, db_acc,
    back, db_send, db_core, db_keep, db_in, db_part, db_whole, db_final,
    load, qg_send, qg_recv, qg_local, t_send, t_recv, t_local,
    r_send, r_recv, s_send, s_recv, a_send, a_recv,
    bp_send, bp_recv, by_send, by_recv, bc_send, bc_recv,
    dc_send, dc_recv, dy_send, dy_recv, dh_send, dh_recv,
    e_send, e_recv, e_local, h_local,
):
    ny, nxh, nz = geometry
    nx = 2 * nxh
    row = lax.axis_index("row")
    col = lax.axis_index("col")
    y, xh = lax.div(row, nxh), lax.rem(row, nxh)
    z, quad = lax.div(col, 4), lax.rem(col, 4)
    xl, core = lax.div(quad, 2), lax.rem(quad, 2)
    x = xh * 2 + xl
    right, left = lax.rem(z + 1, nz), lax.rem(z + nz - 1, nz)
    right_id = {"col": right * 4 + quad}
    left_id = {"col": left * 4 + quad}
    quad_of = [lax.rem(quad + o, 4) for o in range(1, 4)]
    quad_ids = [{"col": z * 4 + p} for p in quad_of]
    plane_ids = []
    for o in range(1, nx * ny):
        px, py = lax.rem(x + o % nx, nx), lax.rem(y + o // nx, ny)
        plane_ids.append({"row": py * nxh + lax.div(px, 2), "col": z * 4 + lax.rem(px, 2) * 2 + core})
    core_id = {"col": z * 4 + xl * 2 + 1 - core}
    chips = nx * ny
    deep = 16 * max(1, 12 // chips)
    owners, pieces = 192 // deep, 48 // deep
    chip = row * 2 + xl
    active = chip < owners
    own_rows = pl.ds(pl.multiple_of(jnp.where(active, chip, 0) * deep, deep), deep)
    origin = lax.div(jnp.where(active, chip, 0) * deep, 48)
    own_piece = jnp.logical_and(jnp.logical_and(row == z, active), origin == quad)
    home_step = jnp.where(xl == 0, lax.rem(row - z + nz, nz), lax.rem(z - row + nz, nz))
    owner_ids = []
    for m in range(pieces):
        for c in range(2):
            at = quad * pieces + m
            owner_ids.append((
                m, c, jnp.logical_and(own_piece, jnp.logical_and(at == chip, core == c)),
                {"row": lax.div(at, 2), "col": row * 4 + lax.rem(at, 2) * 2 + c},
            ))

    def home_of(s):
        at = jnp.where(origin < 2, z + nz - s, z + s)
        return {"row": z, "col": lax.rem(at, nz) * 4 + origin}

    loads = [
        pltpu.make_async_copy(source, target, load.at[at])
        for at, (source, target) in enumerate(
            [(bias_ref, bias_own), (g_ref, g_own), (o_ref, o_own), (ln_ref, ln_own), (mask_ref, mask_own)]
        )
    ]
    for copy in loads:
        copy.start()

    barrier = pltpu.get_barrier_semaphore()
    greeted = quad_ids + [right_id, left_id] + plane_ids
    for peer in greeted:
        pl.semaphore_signal(barrier, inc=1, device_id=peer, device_id_type=MESH)

    for _, _, same, peer in owner_ids:
        @pl.when(jnp.logical_not(same))
        def _():
            pl.semaphore_signal(barrier, inc=1, device_id=peer, device_id_type=MESH)

    for s in range(nz):
        @pl.when(jnp.logical_and(active, jnp.logical_not(jnp.logical_and(own_piece, s == 0))))
        def _():
            pl.semaphore_signal(barrier, inc=1, device_id=home_of(s), device_id_type=MESH)

    loads[0].wait()
    lanes = jnp.concatenate([bias_own[h] for h in range(HEADS)], axis=1)
    bias_wide[0] = lanes[:, :384]
    bias_wide[1] = lanes[:, 384:]

    for copy in loads[1:]:
        copy.wait()
    lane = iota((48, 128), 1)
    term = lax.rem(lane, 8)
    norm = jnp.concatenate([ln_own[h] for h in range(HEADS)], axis=0) * F32(scaling ** -1)
    norm_terms = [part.astype(BF16) for part in split3(norm)]
    source_lane, target_lane = iota((128, 128), 0), iota((128, 128), 1)
    target_term = lax.rem(target_lane, 8)
    same_head = lax.div(source_lane, 32) == lax.rem(lax.div(target_lane, 8), 4)
    delta_term = jnp.logical_and(target_term >= 3, target_term < 6)
    norm_source, norm_target = iota((64, 128), 0), iota((64, 128), 1)
    norm_row = lax.rem(norm_source, 16)
    norm_fits = jnp.logical_and(
        lax.rem(norm_target, 8) < 3, lax.div(norm_source, 16) == lax.rem(lax.div(norm_target, 8), 4)
    )

    def stats(target, carry):
        total = jnp.zeros((48, 128), F32)
        pick = jnp.where(
            jnp.logical_and(norm_row - target * 4 == lax.div(norm_target, 32), norm_fits), 1.0, 0.0
        ).astype(BF16)
        for part in norm_terms:
            total += lax.dot_general(part, pick, TN, preferred_element_type=F32)
        for i in range(4):
            gather = jnp.where(
                jnp.logical_and(
                    jnp.logical_and(same_head, delta_term), lax.div(target_lane, 32) == i
                ), 1.0, 0.0,
            ).astype(BF16)
            product = g_own[target * 4 + i].astype(F32) * o_own[target * 4 + i].astype(F32)
            high = product.astype(BF16)
            low = (product - high.astype(F32)).astype(BF16)
            total += jnp.dot(high, gather, preferred_element_type=F32)
            total += jnp.dot(low, gather, preferred_element_type=F32)
        high, middle, low = split3(-total)
        value = jnp.where(
            jnp.logical_or(term == 0, term == 3), high,
            jnp.where(jnp.logical_or(term == 1, term == 4), middle,
                      jnp.where(jnp.logical_or(term == 2, term == 5), low,
                                jnp.where(term == 6, 1.0, 0.0))),
        )
        st_out[target] = value.astype(BF16)
        return carry

    lax.fori_loop(0, 4, stats, 0)
    pl.semaphore_wait(barrier,
        len(greeted) + 2 * pieces + jnp.where(active, nz, 0) - jnp.where(own_piece, 2, 0)
    )

    def remote(source, target, send, recv, device):
        return pltpu.make_async_remote_copy(
            src_ref=source, dst_ref=target, send_sem=send, recv_sem=recv,
            device_id=device, device_id_type=MESH,
        )

    place = pl.ds(pl.multiple_of(core * 48, 48), 48)
    mine = pl.ds(pl.multiple_of(quad * 48, 48), 48)

    def swap_row(i, sources):
        kind = 0 if sources is queries_grads else 1
        copies = []
        for at, source in sources:
            target = (qg.at[0, i, xl, at, place, :] if at < 2 else (kx, vx)[at - 2].at[i, mine, :])
            for o in range(3):
                copies.append(remote(
                    source.at[4 * quad_of[o] + i], target,
                    qg_send.at[kind], qg_recv.at[kind, i], quad_ids[o],
                ))
            copies.append(pltpu.make_async_copy(source.at[4 * quad + i], target, qg_local.at[kind, i]))
        return copies

    def swapped(i, kind):
        part = g_own.at[pl.ds(0, 6)]
        remote(part, part, qg_send.at[kind], qg_recv.at[kind, i], core_id).wait_recv()
        part = g_own.at[pl.ds(0, 2)]
        pltpu.make_async_copy(part, part, qg_local.at[kind, i]).wait()

    queries_grads = ((0, q_ref), (1, g_ref))
    keys_values = ((2, k_ref), (3, v_ref))
    for i in range(4):
        for copy in swap_row(i, queries_grads):
            copy.start()

    def push(m, c, peer):
        rows = pl.ds(pl.multiple_of(quad * 48 + m * deep, deep), deep)
        return remote(
            bias_wide.at[c, pl.ds(m * deep, deep)], bias_all.at[home_step, c, rows],
            bp_send.at[m, c], bp_recv.at[home_step], peer,
        )

    for m, c, same, peer in owner_ids:
        @pl.when(jnp.logical_not(same))
        def _():
            push(m, c, peer).start()

        @pl.when(same)
        def _():
            bias_all[0, c, own_rows] = bias_wide[c, m * deep:(m + 1) * deep]

    for i in range(4):
        for copy in swap_row(i, keys_values):
            copy.start()

    def all_of(part, send, recv):
        return remote(part, part, send, recv, core_id)

    def pass_on(s, i):
        return [
            remote(qg.at[s, i, 0], qg.at[s + 1, i, 0], r_send.at[s], r_recv.at[s + 1, i], right_id),
            remote(qg.at[s, i, 1], qg.at[s + 1, i, 1], r_send.at[s], r_recv.at[s + 1, i], left_id),
        ]

    def passed_on(s, i):
        return all_of(qg.at[s + 1, i], r_send.at[s], r_recv.at[s + 1, i])

    def pass_stats(s):
        return [
            remote(st.at[s, 0], st.at[s + 1, 0], s_send.at[s], s_recv.at[s + 1], right_id),
            remote(st.at[s, 1], st.at[s + 1, 1], s_send.at[s], s_recv.at[s + 1], left_id),
        ]

    def passed_stats(s):
        return all_of(st.at[s + 1], s_send.at[s], s_recv.at[s + 1])

    def pass_sum(s, i):
        return [
            remote(acc_out.at[s, i, 0], acc_in.at[s + 1, i, 0], a_send.at[s], a_recv.at[s + 1, i], right_id),
            remote(acc_out.at[s, i, 1], acc_in.at[s + 1, i, 1], a_send.at[s], a_recv.at[s + 1, i], left_id),
        ]

    def passed_sum(s, i):
        return all_of(acc_in.at[s + 1, i], a_send.at[s], a_recv.at[s + 1, i])

    target = st.at[0, xl, place, :]
    stat_swaps = [
        remote(st_out.at[quad_of[o]], target, t_send.at[o], t_recv.at[o], quad_ids[o]) for o in range(3)
    ]
    stat_swaps.append(pltpu.make_async_copy(st_out.at[quad], target, t_local.at[0]))
    for copy in stat_swaps:
        copy.start()

    def clear(s, carry):
        for c in range(2):
            db_acc[s, c] = jnp.zeros((192, 384), F32)
        return carry

    lax.fori_loop(0, nz, clear, 0)

    def start_row(i):
        swapped(i, 0)
        for copy in pass_on(0, i):
            copy.start()

    start_row(0)

    def spread(s):
        @pl.when(active)
        def _():
            part = bias_all.at[s, core, own_rows]

            @pl.when(jnp.logical_not(jnp.logical_and(own_piece, s == 0)))
            def _():
                remote(part, part, bp_send.at[0, 0], bp_recv.at[s], core_id).wait_recv()

            for peer in plane_ids:
                remote(part, part, by_send.at[s], by_recv.at[s], peer).start()

    spread(0)
    start_row(1)
    start_row(2)
    start_row(3)
    for copy in stat_swaps:
        copy.wait()
    for copy in pass_stats(0):
        copy.start()

    wide_lane = iota((192, 128), 1)
    masked = mask_own[:, 0:192]
    for other in range(1, nz):
        masked = jnp.where(z == other, mask_own[:, 192 * other:192 * other + 192], masked)
    masked = jnp.where(masked == 1, 0.0, -BIG).astype(BF16)
    mask_row, mask_lane = iota((16, 128), 0), iota((16, 128), 1)

    def weights(i, carry):
        swapped(i, 1)
        keys, values = kx[i].astype(F32), vx[i].astype(F32)
        pick = jnp.where(
            jnp.logical_and(mask_row == 4 * quad + i, lax.rem(mask_lane, 8) == 6), 1.0, 0.0
        ).astype(BF16)
        mask_lanes = lax.dot_general(masked, pick, TN, preferred_element_type=F32)
        zero = jnp.zeros((192, 128), F32)
        for h in range(HEADS):
            head = lax.div(wide_lane, 32) == h
            block = pl.ds(h * 192, 192)
            offset = wide_lane - (i * 32 + h * 8)
            ws[i, block, 0:128] = jnp.where(head, keys, zero).astype(BF16)
            wp[i, block, 0:128] = jnp.where(head, values, zero).astype(BF16)
            ws[i, block, 128:256] = jnp.where(
                jnp.logical_and(offset >= 0, offset < 3), 1.0, jnp.where(offset == 6, mask_lanes, zero)
            ).astype(BF16)
            wp[i, block, 128:256] = jnp.where(
                jnp.logical_and(offset >= 3, offset < 6), 1.0, zero
            ).astype(BF16)
        ws_t[i] = ws[i].T
        wp_t[i] = wp[i].T
        dk_acc[i] = jnp.zeros(dk_acc.shape[1:], F32)
        dv_acc[i] = jnp.zeros(dv_acc.shape[1:], F32)
        return carry

    def bias_core(s):
        part = bias_all.at[s, core]
        return remote(part, part, bc_send.at[s], bc_recv.at[s], core_id)

    def share_bias(s):
        def gathered(rows):
            part = bias_all.at[s, core, pl.ds(0, rows)]
            remote(part, part, by_send.at[s], by_recv.at[s], core_id).wait_recv()

        pl.when(active)(lambda: gathered(192 - deep))
        pl.when(jnp.logical_not(active))(lambda: gathered(192))
        bias_core(s).start()

    ahead, behind = min(3, nz), min(3, nz)
    for step in range(1, ahead):
        spread(step)
    lax.fori_loop(0, 4, weights, 0)
    for i in range(4):
        passed_on(0, i).wait_recv()
        if nz > 2:
            for copy in pass_on(1, i):
                copy.start()
    share_bias(0)

    def sum_core(s):
        return remote(db_send.at[s], db_core.at[s], dc_send.at[s], dc_recv.at[s], core_id)

    def to_owner(s, c):
        slot = chip - jnp.where(chip > c, 1, 0)
        return remote(
            db_keep.at[s, pl.ds(c * deep, deep)], db_in.at[s, slot], dy_send.at[s], dy_recv.at[s],
            {"row": c // 2, "col": z * 4 + (c % 2) * 2 + core},
        )

    def to_home(s):
        return remote(
            db_part.at[s], db_whole.at[pl.ds(pl.multiple_of(core * 48 + lax.rem(chip * deep, 48), deep), deep)],
            dh_send.at[s], dh_recv.at[0], home_of(s),
        )

    def share_sum(s):
        db_send[s] = db_acc[s, 1 - core].astype(BF16)
        sum_core(s).start()

    def add_cores(s):
        sum_core(s).wait_recv()
        whole = db_acc[s, core] + db_core[s].astype(F32)
        db_acc[s, core] = whole
        db_keep[s] = whole.astype(BF16)
        for c in range(owners):
            @pl.when(c != chip)
            def _():
                to_owner(s, c).start()

    def add_chips(s):
        @pl.when(active)
        def _():
            remote(db_in.at[s], db_in.at[s], dy_send.at[s], dy_recv.at[s], core_id).wait_recv()
            whole = db_acc[s, core, own_rows]
            for o in range(chips - 1):
                whole = whole + db_in[s, o].astype(F32)
            own = jnp.logical_and(own_piece, s == 0)

            @pl.when(own)
            def _():
                db_whole[pl.ds(pl.multiple_of(core * 48 + lax.rem(chip * deep, 48), deep), deep)] = whole.astype(BF16)

            @pl.when(jnp.logical_not(own))
            def _():
                db_part[s] = whole.astype(BF16)
                to_home(s).start()

    def turned(acc, i, factor):
        blocks = []
        for t in range(3):
            unit = jnp.where(iota((64, 128), 0) + 32 * t == iota((64, 128), 1), 1.0, 0.0).astype(BF16)
            part = (acc[i, t] * F32(factor)).astype(BF16)
            blocks.append(lax.dot_general(part, unit, TN, preferred_element_type=F32))
        stacked = jnp.concatenate(blocks, axis=0)
        total = jnp.zeros((192, 128), F32)
        for h in range(HEADS):
            total = jnp.where(lax.div(wide_lane, 32) == h, stacked[192 * h:192 * h + 192], total)
        return total.astype(BF16)

    outs = (dq_out, dk_out, dv_out)

    def give_back(at, i):
        copies = []
        for o in range(3):
            columns = pl.ds(pl.multiple_of(quad_of[o] * 48, 48), 48)
            copies.append(remote(
                back.at[at, i, columns, :], outs[at].at[4 * quad + i],
                e_send.at[at], e_recv.at[at], quad_ids[o],
            ))
        copies.append(pltpu.make_async_copy(back.at[at, i, mine, :], outs[at].at[4 * quad + i], e_local.at[at]))
        return copies

    split = (
        ((0, slice(0, 256)),), ((0, slice(256, 384)), (1, slice(0, 128))), ((1, slice(128, 384)),)
    )

    def two_rows(s, p):
        rows = [2 * p, 2 * p + 1]
        terms = jnp.concatenate([st[s, 0], st[s, 1]], axis=0)
        sides = []
        for i in rows:
            queries = jnp.concatenate([qg[s, i, 0, 0], qg[s, i, 1, 0]], axis=0)
            grads = jnp.concatenate([qg[s, i, 0, 1], qg[s, i, 1, 1]], axis=0)
            sides.append((
                jnp.concatenate([queries, terms], axis=1), jnp.concatenate([grads, terms], axis=1),
                queries.T, grads.T,
            ))
        grad_queries = [jnp.zeros((192, 128), F32) for _ in rows]
        for t in range(3):
            span = pl.ds(256 * t, 256)
            part = slice(32 * t, 32 * t + 64)
            bias = jnp.concatenate([bias_all[s, c, :, lanes] for c, lanes in split[t]], axis=1).astype(F32)
            both = None
            for r, i in enumerate(rows):
                left_s, left_p, queries_t, grads_t = sides[r]
                logits = jnp.dot(left_s, ws_t[i, :, span], preferred_element_type=F32)
                prob_grad = jnp.dot(left_p, wp_t[i, :, span], preferred_element_type=F32)
                probs = jnp.exp(logits * F32(scaling) + bias)
                score_grad = probs * prob_grad
                probs_low = probs.astype(BF16)
                score_low = score_grad.astype(BF16)
                both = score_grad if both is None else both + score_grad
                grad_queries[r] += jnp.dot(score_low, ws[i, span, 0:128], preferred_element_type=F32)
                dk_acc[i, t] += jnp.dot(queries_t[part], score_low, preferred_element_type=F32)
                dv_acc[i, t] += jnp.dot(grads_t[part], probs_low, preferred_element_type=F32)
            begin = 0
            for c, lanes in split[t]:
                width = lanes.stop - lanes.start
                db_acc[s, c, :, lanes] += both[:, begin:begin + width]
                begin += width

        @pl.when(s < nz - 2)
        def _():
            for i in rows:
                passed_on(s + 1, i).wait_recv()

                @pl.when(s < nz - 3)
                def _():
                    for copy in pass_on(s + 2, i):
                        copy.start()

        @pl.when(s == 0)
        def _():
            for i, grad_query in zip(rows, grad_queries):
                dq_own[i] = grad_query

        @pl.when(s == 1)
        def _():
            for i, grad_query in zip(rows, grad_queries):
                acc_out[1, i, 0] = grad_query[:96].astype(BF16)
                acc_out[1, i, 1] = grad_query[96:].astype(BF16)

        @pl.when(s > 1)
        def _():
            for i, grad_query in zip(rows, grad_queries):
                passed_sum(s - 1, i).wait_recv()
                acc_out[s, i, 0] = (grad_query[:96] + acc_in[s, i, 0].astype(F32)).astype(BF16)
                acc_out[s, i, 1] = (grad_query[96:] + acc_in[s, i, 1].astype(F32)).astype(BF16)

        @pl.when(s > 0)
        def _():
            for i in rows:
                for copy in pass_sum(s, i):
                    copy.start()

        @pl.when(s == nz - 1)
        def _():
            for i in rows:
                back[1, i] = turned(dk_acc, i, scaling)
                back[2, i] = turned(dv_acc, i, 1.0)
                for at in (1, 2):
                    for copy in give_back(at, i):
                        copy.start()

    def one_step(s, carry):
        bias_core(s).wait_recv()

        def pair(p, inner):
            two_rows(s, p)

            @pl.when(jnp.logical_and(p == 0, s > 0))
            def _():
                add_cores(s - 1)

            @pl.when(jnp.logical_and(p == 0, s < nz - 1))
            def _():
                share_bias(s + 1)

            @pl.when(jnp.logical_and(p == 0, s < nz - ahead))
            def _():
                spread(s + ahead)

            @pl.when(jnp.logical_and(p == 1, s >= behind))
            def _():
                add_chips(s - behind)

            return inner

        lax.fori_loop(0, 2, pair, 0)
        share_sum(s)

        @pl.when(s < nz - 1)
        def _():
            passed_stats(s).wait_recv()

            @pl.when(s < nz - 2)
            def _():
                for copy in pass_stats(s + 1):
                    copy.start()

        return carry

    lax.fori_loop(0, nz, one_step, 0)

    def finish_query(i, carry):
        passed_sum(nz - 1, i).wait_recv()
        for w in range(2):
            part = pl.ds(96 * w, 96)
            whole = dq_own[i, part, :] + acc_in[nz, i, w].astype(F32)
            back[0, i, part, :] = (whole * F32(scaling)).astype(BF16)
        for copy in give_back(0, i):
            copy.start()
        return carry

    add_cores(nz - 1)
    for step in range(nz - behind, nz - 1):
        add_chips(step)
    lax.fori_loop(0, 4, finish_query, 0)
    add_chips(nz - 1)

    def sent(s, carry):
        @pl.when(s < nz - 1)
        def _():
            all_of(qg.at[s], r_send.at[s], r_recv.at[s, 0]).wait_send()
            passed_stats(s).wait_send()

        @pl.when(s > 0)
        def _():
            all_of(acc_out.at[s], a_send.at[s], a_recv.at[s, 0]).wait_send()

        bias_core(s).wait_send()
        sum_core(s).wait_send()

        @pl.when(active)
        def _():
            remote(db_in.at[s], db_in.at[s], by_send.at[s], by_recv.at[s], core_id).wait_send()
            pl.when(jnp.logical_not(jnp.logical_and(own_piece, s == 0)))(to_home(s).wait_send)

        def passed(rows):
            part = db_keep.at[s, pl.ds(0, rows)]
            remote(part, part, dy_send.at[s], dy_recv.at[s], core_id).wait_send()

        pl.when(active)(lambda: passed(192 - deep))
        pl.when(jnp.logical_not(active))(lambda: passed(192))

        return carry

    lax.fori_loop(0, nz, sent, 0)
    for m, c, same, peer in owner_ids:
        pl.when(jnp.logical_not(same))(push(m, c, peer).wait_send)

    for kind in range(2):
        all_of(g_own.at[pl.ds(0, 12)], qg_send.at[kind], qg_recv.at[kind, 0]).wait_send()
        all_of(g_own.at[pl.ds(0, 12)], qg_send.at[kind], qg_recv.at[kind, 0]).wait_send()
    for at in range(3):
        all_of(back.at[at, pl.ds(0, 3)], e_send.at[at], e_recv.at[at]).wait()
        pltpu.make_async_copy(back.at[at, 0], back.at[at, 0], e_local.at[at]).wait()

    def arrived(rows):
        part = db_whole.at[pl.ds(0, rows)]
        remote(part, part, dh_send.at[0], dh_recv.at[0], core_id).wait_recv()

    pl.when(own_piece)(lambda: arrived(96 - deep))
    pl.when(jnp.logical_not(own_piece))(lambda: arrived(96))
    total = jnp.concatenate([db_whole[0:48], db_whole[48:96]], axis=1).astype(F32)
    for h in range(HEADS):
        db_final[h] = total[:, 192 * h:192 * h + 192].astype(BF16)
    final = pltpu.make_async_copy(db_final, db_out, h_local.at[0])
    final.start()
    final.wait()


def solution(mesh):
    rows_n, cols_n = mesh.shape["row"], mesh.shape["col"]
    nz = cols_n // 4
    nxh = 2 if rows_n >= 4 else 1
    ny = rows_n // nxh
    nx = 2 * nxh
    deep = 16 * max(1, 12 // (nx * ny))

    def shards(query_proj, key_proj, value_proj, attn_out, out_grad, log_norm, pair_mask, pair_bias):
        width = query_proj.shape[2]
        scaling = (width // HEADS) ** -0.5
        anywhere = pl.BlockSpec(memory_space=pl.ANY)
        dma = pltpu.SemaphoreType.DMA
        shapes = (
            jax.ShapeDtypeStruct((16, 48, 128), BF16),
            jax.ShapeDtypeStruct((16, 48, 128), BF16),
            jax.ShapeDtypeStruct((16, 48, 128), BF16),
            jax.ShapeDtypeStruct((HEADS, 48, 192), BF16),
        )
        results = pl.pallas_call(
            functools.partial(kernel, (ny, nxh, nz), scaling),
            out_shape=tuple(pltpu.VMEM(shape.shape, shape.dtype) for shape in shapes),
            in_specs=[anywhere] * 8,
            out_specs=(pl.BlockSpec(memory_space=pltpu.VMEM),) * 4,
            scratch_shapes=[
                pltpu.VMEM((16, 48, 128), BF16),
                pltpu.VMEM((16, 48, 128), BF16),
                pltpu.VMEM((HEADS, 16, 48), F32),
                pltpu.VMEM((16, nz * 192), jnp.int32),
                pltpu.VMEM((HEADS, 48, 192), BF16),
                pltpu.VMEM((2, 48, 384), BF16),
                pltpu.VMEM((nz, 4, 2, 2, 96, 128), BF16),
                pltpu.VMEM((nz, 2, 96, 128), BF16),
                pltpu.VMEM((4, 48, 128), BF16),
                pltpu.VMEM((4, 192, 128), BF16),
                pltpu.VMEM((4, 192, 128), BF16),
                pltpu.VMEM((4, 768, 256), BF16),
                pltpu.VMEM((4, 768, 256), BF16),
                pltpu.VMEM((4, 256, 768), BF16),
                pltpu.VMEM((4, 256, 768), BF16),
                pltpu.VMEM((nz, 2, 192, 384), BF16),
                pltpu.VMEM((nz + 1, 4, 2, 96, 128), BF16),
                pltpu.VMEM((nz, 4, 2, 96, 128), BF16),
                pltpu.VMEM((4, 192, 128), F32),
                pltpu.VMEM((4, 3, 64, 256), F32),
                pltpu.VMEM((4, 3, 64, 256), F32),
                pltpu.VMEM((nz, 2, 192, 384), F32),
                pltpu.VMEM((3, 4, 192, 128), BF16),
                pltpu.VMEM((nz, 192, 384), BF16),
                pltpu.VMEM((nz, 192, 384), BF16),
                pltpu.VMEM((nz, 192, 384), BF16),
                pltpu.VMEM((nz, nx * ny - 1, deep, 384), BF16),
                pltpu.VMEM((nz, deep, 384), BF16),
                pltpu.VMEM((96, 384), BF16),
                pltpu.VMEM((HEADS, 48, 192), BF16),
                dma((5,)),
                dma((2,)), dma((2, 4)), dma((2, 4)),
                dma((3,)), dma((3,)), dma((1,)),
                dma((nz,)), dma((nz, 4)),
                dma((nz,)), dma((nz,)),
                dma((nz,)), dma((nz + 1, 4)),
                dma((48 // deep, 2)), dma((nz,)),
                dma((nz,)), dma((nz,)),
                dma((nz,)), dma((nz,)),
                dma((nz,)), dma((nz,)),
                dma((nz,)), dma((nz,)),
                dma((nz,)), dma((1,)),
                dma((3,)), dma((3,)), dma((3,)),
                dma((1,)),
            ],
            compiler_params=pltpu.CompilerParams(
                collective_id=0, has_side_effects=True, vmem_limit_bytes=56 * 1024 * 1024
            ),
        )(query_proj, key_proj, value_proj, attn_out, out_grad, log_norm, pair_mask, pair_bias)
        return results

    placed = (
        P("row", "col", None), P("row", "col", None), P("row", "col", None), P("row", "col", None),
        P("row", "col", None), P(None, "row", "col"), P("row", None), P(None, "col", "row"),
    )
    return jax.shard_map(
        shards,
        mesh=mesh,
        in_specs=placed,
        out_specs=(P("row", "col", None), P("row", "col", None), P("row", "col", None), P(None, "col", "row")),
        check_vma=False,
    )
```

profile of v0, /device:TPU:6, one launch (start us, length us, event | category | flops | bytes accessed | tf_op | source)
XLA Modules:
  0.0 94.2 jit_solution(1798002626673483744)
XLA Ops:
  0.6 90.9 %shard_map.111 = (bf16[16,48,128]{2,1,0:T(8,128)(2,1)S(1)}, bf16[16,48,128]{2,1,0:T(8,128)(2,1)S(1)}, bf16[16,48,128]{2,1,0:T(8,128)(2,1)S(1)}, bf16[4,48,192]{2,1,0:T(8,128)(2,1)S(1)}) custom-call(bf16[16,48,128]{2,1,0:T(8,128)(2,1)} %q_ref.1, bf16[16,48,128]{2,1,0:T(8,128)(2,1)} %k_ref.1, bf16[16,48,128]{2,1,0:T(8,128)(2,1)} %v_ref.1, ...), custom_call_target="tpu_custom_call" | custom-call | tf_op jit(solution)/shard_map/pallas_call | solution.py:629
  91.5 0.7 copy.16
  92.2 0.6 copy.19
  92.8 0.7 copy.17
  93.5 0.7 copy.18
where the time goes:
time: 94.3 us; the launch traced here: 94.2 us
  Pallas kernels  90.9 us (96%)
  local copies, waits for them, and re-layouts  2.67 us (3%)
    pallas_call x1, Pallas kernels, shards(): pl.pallas_call(functools.partial(kernel, (ny, nxh, nz), scaling), out_sha...  90.9 us
    unnamed x4, local copies, waits for them, and re-layouts  2.67 us

commit v1 on v0

--- a/solution.py
+++ b/solution.py
@@ -33,7 +33,7 @@
     q_ref, k_ref, v_ref, o_ref, g_ref, ln_ref, mask_ref, bias_ref,
     dq_out, dk_out, dv_out, db_out,
     o_own, g_own, ln_own, mask_own, bias_own, bias_wide,
-    qg, st, st_out, kx, vx, ws, wp, ws_t, wp_t, bias_all,
+    qg, st, st_in, st_two, st_out, kx, vx, ws, wp, ws_t, wp_t, bias_all,
     acc_in, acc_out, dq_own, dk_acc, dv_acc, db_acc,
     back, db_send, db_core, db_keep, db_in, db_part, db_whole, db_final,
     load, qg_send, qg_recv, qg_local, t_send, t_recv, t_local,
@@ -114,30 +114,29 @@
     for copy in loads[1:]:
         copy.wait()
     lane = iota((48, 128), 1)
-    term = lax.rem(lane, 8)
+    term = lax.rem(lane, 4)
     norm = jnp.concatenate([ln_own[h] for h in range(HEADS)], axis=0) * F32(scaling ** -1)
     norm_terms = [part.astype(BF16) for part in split3(norm)]
     source_lane, target_lane = iota((128, 128), 0), iota((128, 128), 1)
-    target_term = lax.rem(target_lane, 8)
-    same_head = lax.div(source_lane, 32) == lax.rem(lax.div(target_lane, 8), 4)
-    delta_term = jnp.logical_and(target_term >= 3, target_term < 6)
+    same_head = lax.div(source_lane, 32) == lax.rem(lax.div(target_lane, 4), 4)
+    delta_term = lax.rem(target_lane, 4) >= 2
     norm_source, norm_target = iota((64, 128), 0), iota((64, 128), 1)
     norm_row = lax.rem(norm_source, 16)
     norm_fits = jnp.logical_and(
-        lax.rem(norm_target, 8) < 3, lax.div(norm_source, 16) == lax.rem(lax.div(norm_target, 8), 4)
+        lax.rem(norm_target, 4) < 2, lax.div(norm_source, 16) == lax.rem(lax.div(norm_target, 4), 4)
     )
 
     def stats(target, carry):
         total = jnp.zeros((48, 128), F32)
         pick = jnp.where(
-            jnp.logical_and(norm_row - target * 4 == lax.div(norm_target, 32), norm_fits), 1.0, 0.0
+            jnp.logical_and(norm_row - target * 4 == lax.div(norm_target, 16), norm_fits), 1.0, 0.0
         ).astype(BF16)
         for part in norm_terms:
             total += lax.dot_general(part, pick, TN, preferred_element_type=F32)
         for i in range(4):
             gather = jnp.where(
                 jnp.logical_and(
-                    jnp.logical_and(same_head, delta_term), lax.div(target_lane, 32) == i
+                    jnp.logical_and(same_head, delta_term), lax.div(target_lane, 16) == i
                 ), 1.0, 0.0,
             ).astype(BF16)
             product = g_own[target * 4 + i].astype(F32) * o_own[target * 4 + i].astype(F32)
@@ -145,13 +144,9 @@
             low = (product - high.astype(F32)).astype(BF16)
             total += jnp.dot(high, gather, preferred_element_type=F32)
             total += jnp.dot(low, gather, preferred_element_type=F32)
-        high, middle, low = split3(-total)
-        value = jnp.where(
-            jnp.logical_or(term == 0, term == 3), high,
-            jnp.where(jnp.logical_or(term == 1, term == 4), middle,
-                      jnp.where(jnp.logical_or(term == 2, term == 5), low,
-                                jnp.where(term == 6, 1.0, 0.0))),
-        )
+        high, middle, _ = split3(-total)
+        value = jnp.where(lax.rem(term, 2) == 0, high, middle)
+        value = jnp.where(lane < 64, value, 0.0)
         st_out[target] = value.astype(BF16)
         return carry
 
@@ -244,7 +239,7 @@
     def passed_sum(s, i):
         return all_of(acc_in.at[s + 1, i], a_send.at[s], a_recv.at[s + 1, i])
 
-    target = st.at[0, xl, place, :]
+    target = st_in.at[xl, place, :]
     stat_swaps = [
         remote(st_out.at[quad_of[o]], target, t_send.at[o], t_recv.at[o], quad_ids[o]) for o in range(3)
     ]
@@ -284,6 +279,9 @@
     start_row(3)
     for copy in stat_swaps:
         copy.wait()
+    for w in range(2):
+        upper = pltpu.roll(st_in[w, 48:96, :].astype(F32), 64, 1)
+        st[0, w] = jnp.where(lane < 64, st_in[w, 0:48, :].astype(F32), upper).astype(BF16)
     for copy in pass_stats(0):
         copy.start()
 
@@ -298,21 +296,21 @@
         swapped(i, 1)
         keys, values = kx[i].astype(F32), vx[i].astype(F32)
         pick = jnp.where(
-            jnp.logical_and(mask_row == 4 * quad + i, lax.rem(mask_lane, 8) == 6), 1.0, 0.0
+            jnp.logical_and(mask_row == 4 * quad + i, mask_lane == 64), 1.0, 0.0
         ).astype(BF16)
         mask_lanes = lax.dot_general(masked, pick, TN, preferred_element_type=F32)
         zero = jnp.zeros((192, 128), F32)
         for h in range(HEADS):
             head = lax.div(wide_lane, 32) == h
             block = pl.ds(h * 192, 192)
-            offset = wide_lane - (i * 32 + h * 8)
+            offset = wide_lane - (i * 16 + h * 4)
             ws[i, block, 0:128] = jnp.where(head, keys, zero).astype(BF16)
             wp[i, block, 0:128] = jnp.where(head, values, zero).astype(BF16)
             ws[i, block, 128:256] = jnp.where(
-                jnp.logical_and(offset >= 0, offset < 3), 1.0, jnp.where(offset == 6, mask_lanes, zero)
+                jnp.logical_and(offset >= 0, offset < 2), 1.0, mask_lanes
             ).astype(BF16)
             wp[i, block, 128:256] = jnp.where(
-                jnp.logical_and(offset >= 3, offset < 6), 1.0, zero
+                jnp.logical_and(offset >= 2, offset < 4), 1.0, zero
             ).astype(BF16)
         ws_t[i] = ws[i].T
         wp_t[i] = wp[i].T
@@ -423,7 +421,7 @@
 
     def two_rows(s, p):
         rows = [2 * p, 2 * p + 1]
-        terms = jnp.concatenate([st[s, 0], st[s, 1]], axis=0)
+        terms = st_two[...]
         sides = []
         for i in rows:
             queries = jnp.concatenate([qg[s, i, 0, 0], qg[s, i, 1, 0]], axis=0)
@@ -500,6 +498,12 @@
                         copy.start()
 
     def one_step(s, carry):
+        for w in range(2):
+            packed = st[s, w].astype(F32)
+            for c, part in enumerate((packed, pltpu.roll(packed, 64, 1))):
+                part = jnp.where(lane < 64, part, jnp.where(lane == 64, 1.0, 0.0))
+                st_two[96 * w + 48 * c:96 * w + 48 * c + 48, :] = part.astype(BF16)
+
         bias_core(s).wait_recv()
 
         def pair(p, inner):
@@ -639,7 +643,9 @@
                 pltpu.VMEM((HEADS, 48, 192), BF16),
                 pltpu.VMEM((2, 48, 384), BF16),
                 pltpu.VMEM((nz, 4, 2, 2, 96, 128), BF16),
-                pltpu.VMEM((nz, 2, 96, 128), BF16),
+                pltpu.VMEM((nz, 2, 48, 128), BF16),
+                pltpu.VMEM((2, 96, 128), BF16),
+                pltpu.VMEM((192, 128), BF16),
                 pltpu.VMEM((4, 48, 128), BF16),
                 pltpu.VMEM((4, 192, 128), BF16),
                 pltpu.VMEM((4, 192, 128), BF16),

time: 94.3 us -> 93.4 us (level)
  no operation moved by 1% of the time
where the time goes in v1:
time: 93.4 us; the launch traced here: 93.3 us
  Pallas kernels  90 us (96%)
  local copies, waits for them, and re-layouts  2.67 us (3%)
    pallas_call x1, Pallas kernels, shards(): pl.pallas_call(functools.partial(kernel, (ny, nxh, nz), scaling), out_sha...  90 us
    unnamed x4, local copies, waits for them, and re-layouts  2.67 us

profile of v1, /device:TPU:6, one launch (start us, length us, event | category | flops | bytes accessed | tf_op | source)
XLA Modules:
  0.0 93.3 jit_solution(9704453755888477715)
XLA Ops:
  0.6 90.0 %shard_map.111 = (bf16[16,48,128]{2,1,0:T(8,128)(2,1)S(1)}, bf16[16,48,128]{2,1,0:T(8,128)(2,1)S(1)}, bf16[16,48,128]{2,1,0:T(8,128)(2,1)S(1)}, bf16[4,48,192]{2,1,0:T(8,128)(2,1)S(1)}) custom-call(bf16[16,48,128]{2,1,0:T(8,128)(2,1)} %q_ref.1, bf16[16,48,128]{2,1,0:T(8,128)(2,1)} %k_ref.1, bf16[16,48,128]{2,1,0:T(8,128)(2,1)} %v_ref.1, ...), custom_call_target="tpu_custom_call" | custom-call | tf_op jit(solution)/shard_map/pallas_call | solution.py:633
  90.6 0.7 copy.16
  91.3 0.6 copy.19
  92.0 0.7 copy.17
  92.6 0.7 copy.18
